TPU v7x, 512 devices: a whole 4x8x8 slice. The times are simulated.
512 devices in a mesh: grp: 16 (over y_hi, x), dev: 32 (over z, y_lo, core).
Axes of the slice: x: 4, y: 8 (y_hi: 4, y_lo: 2; y = y_hi * 2 + y_lo), z: 8, core: 2. Of those that a mesh axis runs over, the one named last changes fastest.
Arguments:
- amplitudes: float32 [16, 32, 8, 256, 256], P('grp', 'dev'), may hold values from -6 to 6
- joined_gates: float32 [3, 2, 256, 256], replicated, may hold values from -0.375 to 0.375
- pair_qubits: int32 [3, 8, 2], replicated, may hold values from 0 to 18, as said below
Outputs:
- final_state: float32 [16, 32, 8, 256, 256], P('grp', 'dev')
Inputs may be any that keep to these rules, and one draw needn't show every extreme that they name: `pair_qubits`: in each layer the 16 qubit numbers are all different and are bits of the last three indices; every layer names both 0 and 18.
All inputs are finite; a program needn't handle non-finite values.
Results may differ from a plain program's by a relative error of at most 0.000098.
Values sent between devices are 32-bit elements; how exact they have to be, the bound alone decides.
A program may use at most 64 MiB of HBM per device.

v0:
```python
import jax
import jax.numpy as jnp
from jax import lax
from jax.sharding import PartitionSpec as P


def sign_of(flat_index, pair_row):
    parity = jnp.zeros_like(flat_index)
    for number in range(pair_row.shape[0]):
        bit_one = jnp.right_shift(flat_index, pair_row[number, 0])
        bit_two = jnp.right_shift(flat_index, pair_row[number, 1])
        parity = parity + (bit_one & bit_two & 1)
    return (1 - 2 * (parity & 1)).astype(jnp.float32)


def apply_signs(current, pair_row, swapped):
    devs = lax.axis_size("dev")
    grps = lax.axis_size("grp")
    grp_idx = lax.axis_index("grp")
    dev_idx = lax.axis_index("dev")
    levels = current.shape[2]
    width = current.shape[3]
    grid_shape = (levels, width, width)
    level_pos = lax.broadcasted_iota(jnp.int32, grid_shape, 0)
    middle = lax.broadcasted_iota(jnp.int32, grid_shape, 1)
    column = lax.broadcasted_iota(jnp.int32, grid_shape, 2)
    mid_low = width // devs
    last_low = width // grps
    if swapped:
        dev_pos = middle // mid_low
        middle = dev_idx * mid_low + middle % mid_low
        grp_pos = column // last_low
        column = grp_idx * last_low + column % last_low
    else:
        dev_pos = dev_idx
        grp_pos = grp_idx
    flat_index = (
        ((grp_pos * devs + dev_pos) * levels + level_pos) * width + middle
    ) * width + column
    return current * sign_of(flat_index, pair_row)[None, None]


def along_middle(current, matrix):
    return jnp.einsum("ik,xyhkj->xyhij", matrix, current, precision=lax.Precision.HIGHEST)


def along_last(current, matrix):
    return jnp.einsum("jk,xyhik->xyhij", matrix, current, precision=lax.Precision.HIGHEST)


def swap_devices(current, matrix):
    return along_middle(
        lax.all_to_all(current, "dev", split_axis=3, concat_axis=3, tiled=True), matrix
    )


def swap_groups(current, matrix):
    return along_last(
        lax.all_to_all(current, "grp", split_axis=4, concat_axis=4, tiled=True), matrix
    )


def per_device(amplitudes, joined_gates, pair_qubits):
    current = apply_signs(amplitudes, pair_qubits[0], False)
    current = along_last(along_middle(current, joined_gates[0, 0]), joined_gates[0, 1])
    current = apply_signs(current, pair_qubits[1], False)
    current = swap_devices(current, joined_gates[1, 0])
    current = swap_groups(current, joined_gates[1, 1])
    current = apply_signs(current, pair_qubits[2], True)
    current = swap_groups(current, joined_gates[2, 1])
    current = swap_devices(current, joined_gates[2, 0])
    return current


def solution(mesh):
    placed = (P("grp", "dev", None, None, None), P(), P())
    return jax.shard_map(
        per_device,
        mesh=mesh,
        in_specs=placed,
        out_specs=P("grp", "dev", None, None, None),
        check_vma=False,
    )
```

profile of v0, /device:TPU:1, one launch (start us, length us, event | category | flops | bytes accessed | tf_op | source)
XLA Modules:
  0.0 317.7 jit_solution(2630183916972596666)
XLA Ops:
  0.0 0.7 slice_bitcast_fusion
  0.7 0.7 fusion.118
  1.4 0.7 fusion.117
  2.2 18.2 %fusion.10 = f32[8,256,256]{2,1,0:T(8,128)S(1)} fusion(f32[1,1,8,256,256]{4,3,2,1,0:T(8,128)} %param.3, s32[]{:T(128)} %bitcast.16, s32[]{:T(128)} %bitcast.15, s32[]{:T(128)} %bitcast.14, s32[]{:T(128)} %bitcast.13, s32[]{:T(128)} %bitcast.12, s32[]{:T(128)} %bitcast.11, s32[]{:T(128)} %bitcast.10, s32[]{:T(128)} %bitcast.9, s32[]{:T(128)} %bitcast.8, ...), kind=kOutput, calls=%fused_computation.10 | convolution fusion | flops 1635254272 | bytes 4464672 | tf_op jit(solution)/shard_map/ik,xyhkj->xyhij/dot_general | solution.py:44
  20.4 17.8 %multiply_bitcast_fusion.1 = f32[1,1,8,256,256]{4,3,2,1,0:T(8,128)S(1)} fusion(f32[8,256,256]{2,1,0:T(8,128)S(1)} %fusion.10, s32[]{:T(128)} %bitcast.41, s32[]{:T(128)} %bitcast.40, s32[]{:T(128)} %bitcast.39, s32[]{:T(128)} %bitcast.38, s32[]{:T(128)} %bitcast.37, s32[]{:T(128)} %bitcast.36, s32[]{:T(128)} %bitcast.35, s32[]{:T(128)} %bitcast.34, ...), kind=kOutput, calls=%fused_computation.13 | convolution fusion | flops 1635254272 | bytes 4464672 | tf_op jit(solution)/shard_map/jk,xyhik->xyhij/dot_general | solution.py:48
  38.2 1.2 copy.12
  39.4 63.8 %all_to_all.20 = f32[1,1,8,256,256]{4,2,1,0,3:T(8,128)S(1)} all-to-all(f32[1,1,8,256,256]{4,2,1,0,3:T(8,128)S(1)} %copy.12), channel_id=1, replica_groups=mesh['grp'=16,'dev'=32] {'dev'}, dimensions={3} | all-to-all | bytes 4194304 | tf_op jit(solution)/shard_map/all_to_all | solution.py:53
  103.2 1.8 copy.13
  105.0 3.5 %fusion.61 = f32[1,1,8,256,256]{3,4,2,1,0:T(8,128)S(1)} fusion(f32[1,1,8,256,256]{3,4,2,1,0:T(8,128)} %copy.13, f32[3,2,256,256]{3,2,1,0:T(8,128)} %param.4), kind=kOutput, calls=%fused_computation.63 | convolution fusion | flops 1610612736 | bytes 4456448 | tf_op jit(solution)/shard_map/ik,xyhkj->xyhij/dot_general | solution.py:44
  108.5 2.5 copy.14
  111.1 8.5 %all-to-all-start.1 = ((f32[1,1,8,256,256]{3,2,1,0,4:T(8,128)}), f32[1,1,8,256,256]{3,2,1,0,4:T(8,128)S(1)}, u32[]{:S(2)}, u32[]{:S(2)}) async-start(f32[1,1,8,256,256]{3,2,1,0,4:T(8,128)} %copy.14), calls=%async_computation.1 | async-start | bytes 4194304 | tf_op jit(solution)/shard_map/all_to_all | solution.py:59
  119.6 0.7 fusion.116
  120.4 38.5 %all-to-all-done.1 = f32[1,1,8,256,256]{3,2,1,0,4:T(8,128)S(1)} async-done(((f32[1,1,8,256,256]{3,2,1,0,4:T(8,128)}), f32[1,1,8,256,256]{3,2,1,0,4:T(8,128)S(1)}, u32[]{:S(2)}, u32[]{:S(2)}) %all-to-all-start.1) | async-done | bytes 2097184 | tf_op jit(solution)/shard_map/all_to_all | solution.py:59
  158.9 1.8 copy.15
  160.7 17.2 %multiply_bitcast_fusion = f32[1,1,8,256,256]{4,3,2,1,0:T(8,128)} fusion(f32[1,1,8,256,256]{4,3,2,1,0:T(8,128)} %copy.15, s32[]{:T(128)} %bitcast.67, s32[]{:T(128)} %bitcast.66, s32[]{:T(128)} %bitcast.65, s32[]{:T(128)} %bitcast.64, s32[]{:T(128)} %bitcast.63, s32[]{:T(128)} %bitcast.62, s32[]{:T(128)} %bitcast.61, s32[]{:T(128)} %bitcast.60, ...), kind=kOutput, calls=%fused_computation.12 | convolution fusion | flops 1641021440 | bytes 4473864 | tf_op jit(solution)/shard_map/jk,xyhik->xyhij/dot_general | solution.py:48
  177.9 2.2 copy.16
  180.2 40.5 %all_to_all.21 = f32[1,1,8,256,256]{3,2,1,0,4:T(8,128)} all-to-all(f32[1,1,8,256,256]{3,2,1,0,4:T(8,128)S(1)} %copy.16), channel_id=1, replica_groups=mesh['grp'=16,'dev'=32] {'grp'}, dimensions={4} | all-to-all | bytes 4194304 | tf_op jit(solution)/shard_map/all_to_all | solution.py:59
  220.7 1.9 copy.17
  222.6 2.9 fusion.66
  225.5 1.2 copy.18
  226.7 83.9 %all_to_all.22 = f32[1,1,8,256,256]{4,2,1,0,3:T(8,128)S(1)} all-to-all(f32[1,1,8,256,256]{4,2,1,0,3:T(8,128)S(1)} %copy.18), channel_id=1, replica_groups=mesh['grp'=16,'dev'=32] {'dev'}, dimensions={3} | all-to-all | bytes 4194304 | tf_op jit(solution)/shard_map/all_to_all | solution.py:53
  310.7 1.8 copy.19
  312.5 3.4 %fusion.69 = f32[1,1,8,256,256]{3,4,2,1,0:T(8,128)S(1)} fusion(f32[1,1,8,256,256]{3,4,2,1,0:T(8,128)} %copy.19, f32[3,2,256,256]{3,2,1,0:T(8,128)} %param.4), kind=kOutput, calls=%fused_computation.65 | convolution fusion | flops 1610612736 | bytes 4456448 | tf_op jit(solution)/shard_map/ik,xyhkj->xyhij/dot_general | solution.py:44
  315.9 1.8 copy.20
  (7 shorter events, 0.0 us)
Async XLA Ops:
  111.1 47.8 %all-to-all-start.1 = ((f32[1,1,8,256,256]{3,2,1,0,4:T(8,128)}), f32[1,1,8,256,256]{3,2,1,0,4:T(8,128)S(1)}, u32[]{:S(2)}, u32[]{:S(2)}) async-start(f32[1,1,8,256,256]{3,2,1,0,4:T(8,128)} %copy.14), calls=%async_computation.1 | async-start | bytes 4194304 | tf_op jit(solution)/shard_map/all_to_all | solution.py:59
where the time goes:
time: 319 us; the launch traced here: 318 us
  blocking collectives  188 us (59%)
  matrix products  63.1 us (20%)
  waiting for transfers between devices  38.5 us (12%)
  local copies, waits for them, and re-layouts  19.2 us (6%)
  starting transfers between devices  8.49 us (3%)
    all_to_all x2, blocking collectives, swap_devices(): lax.all_to_all(current, 'dev', split_axis=3, concat_axis=3, tiled=True)  148 us
    all_to_all x1, blocking collectives, swap_groups(): lax.all_to_all(current, 'grp', split_axis=4, concat_axis=4, tiled=True)  40.5 us
    all_to_all x1, waiting for transfers between devices, swap_groups(): lax.all_to_all(current, 'grp', split_axis=4, concat_axis=4, tiled=True)  38.5 us
    dot_general x3, matrix products, along_last(): jnp.einsum('jk,xyhik->xyhij', matrix, current, precision=lax.Precision.HI...  37.9 us
    dot_general x3, matrix products, along_middle(): jnp.einsum('ik,xyhkj->xyhij', matrix, current, precision=lax.Precision.HI...  25.1 us
    all_to_all x1, starting transfers between devices, swap_groups(): lax.all_to_all(current, 'grp', split_axis=4, concat_axis=4, tiled=True)  8.49 us
  transfers between devices with their start and end apart: 1, of which 1 were waited for; matrix products, arithmetic and copies ran while one was open for 0% of the time, Pallas kernels for 0%

commit v1 on v0

v1 whole, which is shorter than its diff:
```python
import functools

import jax
import jax.numpy as jnp
from jax import lax
from jax.sharding import PartitionSpec as P
import jax.experimental.pallas as pl
import jax.experimental.pallas.tpu as pltpu

MESH = pl.DeviceIdType.MESH
GRPS, DEVS = 16, 32
NODES = GRPS * DEVS
HIGH, GATE = 8, 256
NT = (((1,), (1,)), ((), ()))
NN = (((1,), (0,)), ((), ()))


def sign_of(flat, pairs, layer):
    parity = jnp.zeros_like(flat)
    for number in range(8):
        one = jnp.right_shift(flat, pairs[layer, number, 0])
        two = jnp.right_shift(flat, pairs[layer, number, 1])
        parity = parity ^ (one & two)
    return (1 - 2 * (parity & 1)).astype(jnp.float32)


def iota(shape, dim):
    return lax.broadcasted_iota(jnp.int32, shape, dim)


def split(values):
    high = values.astype(jnp.bfloat16)
    low = (values - high.astype(jnp.float32)).astype(jnp.bfloat16)
    return high, low


def split_gate(gate):
    high, low = split(gate)
    return jnp.concatenate([high, high, low], axis=1)


def gates_of(state, middle, last):
    high, low = split(state)
    wide = jnp.concatenate([high, low, high], axis=1)
    half = lax.dot_general(wide, last, NT, preferred_element_type=jnp.float32)
    high, low = split(half)
    tall = jnp.concatenate([high, low, high], axis=0)
    return lax.dot_general(middle, tall, NN, preferred_element_type=jnp.float32)


def regroup(tiles):
    group = iota((8, 128), 1) // 16
    tiles = [pltpu.roll(t, 16 * q, 1) if q else t for q, t in enumerate(tiles)]
    for bit in range(3):
        chosen = (group // 2**bit) % 2 == 1
        tiles = [jnp.where(chosen, tiles[(v + 2**bit) % 8], tiles[v]) for v in range(8)]
    return [pltpu.roll(tiles[8 - p], 128 - 16 * p, 1) if p else tiles[0] for p in range(8)]


def state_to_tiles(state, tiles, sign=None):
    def body(row, carry):
        for half in range(2):
            rows, cols = pl.ds(pl.multiple_of(row * 8, 8), 8), pl.ds(half * 128, 128)
            out = regroup([state[h, rows, cols] for h in range(8)])
            for p in range(8):
                tiles[(half * 8 + p) * DEVS + row] = out[p] if sign is None else out[p] * sign
        return carry

    lax.fori_loop(0, DEVS, body, 0)


def tiles_to_state(tiles, state, sign=None):
    def body(row, carry):
        for half in range(2):
            rows, cols = pl.ds(pl.multiple_of(row * 8, 8), 8), pl.ds(half * 128, 128)
            parts = [tiles[(half * 8 + p) * DEVS + row] for p in range(8)]
            out = regroup(parts if sign is None else [part * sign for part in parts])
            for h in range(8):
                state[h, rows, cols] = out[h]
        return carry

    lax.fori_loop(0, DEVS, body, 0)


def tile_sign(pairs, layer):
    e, f = lax.axis_index("dev"), lax.axis_index("grp")
    lane = iota((8, 128), 1)
    flat = (lane // 16) * 65536 + (e * 8 + iota((8, 128), 0)) * 256 + f * 16 + lane % 16
    return sign_of(flat, pairs, layer)


def first_kernel(pairs, gates, x, tiles, state, row_sign):
    middle, last = split_gate(gates[0, 0]), split_gate(gates[0, 1])
    base = sign_of(iota((GATE, GATE), 0) * 256 + iota((GATE, GATE), 1), pairs, 0)
    rows = iota((GATE, 128), 0) * 256
    row_sign[...] = sign_of((iota((GATE, 128), 1) % 8) * 65536 + rows, pairs, 0) * sign_of(rows, pairs, 0)
    level = iota((8, GATE), 0) * 65536
    column = iota((8, GATE), 1)
    col_sign = (
        sign_of(level + column, pairs, 0) * sign_of(column, pairs, 0) * sign_of(level, pairs, 0)
    )
    for h in range(8):
        signed = x[h] * base * row_sign[:, h : h + 1] * col_sign[h : h + 1, :]
        state[h] = gates_of(signed, middle, last)
    state_to_tiles(state, tiles)


def second_kernel(pairs, gates, got, tiles, state):
    middle, last = split_gate(gates[1, 0]), split_gate(gates[1, 1])
    tiles_to_state(got, state, tile_sign(pairs, 1))
    for h in range(8):
        state[h] = gates_of(state[h], middle, last)
    state_to_tiles(state, tiles, tile_sign(pairs, 2))


def third_kernel(pairs, gates, got, out, state):
    middle, last = split_gate(gates[2, 0]), split_gate(gates[2, 1])
    tiles_to_state(got, state)
    for h in range(8):
        out[h] = gates_of(state[h], middle, last)


def exchange_kernel(src, dst, send_sem, recv_sem, own_sem):
    grp, dev = lax.axis_index("grp"), lax.axis_index("dev")
    x, y, z, core = grp % 4, (grp // 4) * 2 + (dev // 2) % 2, dev // 4, dev % 2
    me = grp * DEVS + dev
    own = pltpu.make_async_copy(src.at[me], dst.at[me], own_sem)
    own.start()

    def body(step, carry):
        mixed = (step * 165) % NODES
        to_x = (x + mixed % 4) % 4
        to_y = (y + (mixed // 4) % 8) % 8
        to_z = (z + (mixed // 32) % 8) % 8
        to_core = (core + mixed // 256) % 2
        to_grp = (to_y // 2) * 4 + to_x
        to_dev = (to_z * 2 + to_y % 2) * 2 + to_core
        pltpu.make_async_remote_copy(
            src_ref=src.at[to_grp * DEVS + to_dev],
            dst_ref=dst.at[me],
            send_sem=send_sem,
            recv_sem=recv_sem,
            device_id=(to_grp, to_dev),
            device_id_type=MESH,
        ).start()
        return carry

    lax.fori_loop(1, NODES, body, 0)
    own.wait()
    others = pl.ds(0, NODES - 1)
    pltpu.make_async_remote_copy(
        src_ref=src.at[others],
        dst_ref=dst.at[others],
        send_sem=send_sem,
        recv_sem=recv_sem,
        device_id=((grp + 1) % GRPS, dev),
        device_id_type=MESH,
    ).wait()


VMEM = pl.BlockSpec(memory_space=pltpu.VMEM)
SMEM = pl.BlockSpec(memory_space=pltpu.SMEM)
TILES = jax.ShapeDtypeStruct((NODES, 8, 128), jnp.float32)
STATE = jax.ShapeDtypeStruct((HIGH, GATE, GATE), jnp.float32)


def compute(kernel, name, out, *scratch):
    return pl.pallas_call(
        kernel,
        out_shape=out,
        in_specs=[SMEM, VMEM, VMEM],
        out_specs=VMEM,
        scratch_shapes=[pltpu.VMEM((HIGH, GATE, GATE), jnp.float32), *scratch],
        name=name,
        compiler_params=pltpu.CompilerParams(vmem_limit_bytes=48 * 2**20),
    )


def exchange(tiles):
    return pl.pallas_call(
        exchange_kernel,
        out_shape=TILES,
        in_specs=[VMEM],
        out_specs=VMEM,
        scratch_shapes=[pltpu.SemaphoreType.DMA] * 3,
        name="exchange",
        compiler_params=pltpu.CompilerParams(
            has_side_effects=True, vmem_limit_bytes=48 * 2**20
        ),
    )(tiles)


def per_device(amplitudes, joined_gates, pair_qubits):
    state = amplitudes.reshape(HIGH, GATE, GATE)
    tiles = compute(first_kernel, "layer_one", TILES, pltpu.VMEM((GATE, 128), jnp.float32))(
        pair_qubits, joined_gates, state
    )
    tiles = exchange(tiles)
    tiles = compute(second_kernel, "layer_two", TILES)(pair_qubits, joined_gates, tiles)
    tiles = exchange(tiles)
    out = compute(third_kernel, "layer_three", STATE)(pair_qubits, joined_gates, tiles)
    return out.reshape(amplitudes.shape)


def solution(mesh):
    placed = (P("grp", "dev", None, None, None), P(), P())
    return jax.shard_map(
        per_device,
        mesh=mesh,
        in_specs=placed,
        out_specs=P("grp", "dev", None, None, None),
        check_vma=False,
    )
```

time: 319 us -> 179 us (0.56)
  blocking collectives: 188 us -> 0 us
  Pallas kernels: 0 us -> 175 us
  matrix products: 63.1 us -> 0 us
  waiting for transfers between devices: 38.5 us -> 0 us
  local copies, waits for them, and re-layouts: 19.2 us -> 3.77 us
  starting transfers between devices: 8.49 us -> 0 us
    all_to_all x3 -> x0, blocking collectives: 188 us -> none  [the longest x2 148 us: swap_devices(): lax.all_to_all(current, 'dev', split_axis=3, concat_axis=3, tiled=True)]
    pallas_call x0 -> x5, Pallas kernels: none -> 175 us  [the longest x2 143 us: exchange(): pl.pallas_call(exchange_kernel, out_shape=TILES, in_specs=[VMEM], out_spe...]
    dot_general x6 -> x0, matrix products: 63.1 us -> none  [the longest x3 37.9 us: along_last(): jnp.einsum('jk,xyhik->xyhij', matrix, current, precision=lax.Precision.HI...]
    all_to_all x1 -> x0, waiting for transfers between devices: 38.5 us -> none  [swap_groups(): lax.all_to_all(current, 'grp', split_axis=4, concat_axis=4, tiled=True)]
    all_to_all x1 -> x0, starting transfers between devices: 8.49 us -> none  [swap_groups(): lax.all_to_all(current, 'grp', split_axis=4, concat_axis=4, tiled=True)]
    all_to_all x4 -> x0, local copies, waits for them, and re-layouts: 7.38 us -> none  [the longest x2 3.75 us: swap_groups(): lax.all_to_all(current, 'grp', split_axis=4, concat_axis=4, tiled=True)]
    transpose x2 -> x0, local copies, waits for them, and re-layouts: 4.35 us -> none  [along_middle(): jnp.einsum('ik,xyhkj->xyhij', matrix, current, precision=lax.Precision.HI...]
    unnamed x0 -> x7, local copies, waits for them, and re-layouts: none -> 3.77 us
  transfers between devices with their start and end apart: 1 -> 0, of which waited for: 1 -> 0; matrix products, arithmetic and copies ran while one was open for 0% -> 0% of each run, Pallas kernels for 0% -> 0%
where the time goes in v1:
time: 179 us; the launch traced here: 178 us
  Pallas kernels  175 us (98%)
  local copies, waits for them, and re-layouts  3.77 us (2%)
    pallas_call x2, Pallas kernels, exchange(): pl.pallas_call(exchange_kernel, out_shape=TILES, in_specs=[VMEM], out_spe...  143 us
    pallas_call x1, Pallas kernels, per_device(): compute(second_kernel, 'layer_two', TILES)(pair_qubits, joined_gates, tiles)  13.4 us
    pallas_call x1, Pallas kernels, per_device(): compute(third_kernel, 'layer_three', STATE)  9.61 us
    pallas_call x1, Pallas kernels, per_device(): compute(first_kernel, 'layer_one', TILES, pltpu.VMEM((GATE, 128), jnp.flo...  8.96 us
    unnamed x7, local copies, waits for them, and re-layouts  3.77 us

profile of v1, /device:TPU:1, one launch (start us, length us, event | category | flops | bytes accessed | tf_op | source)
XLA Modules:
  0.0 178.4 jit_solution(11879359728236626263)
XLA Ops:
  0.0 0.8 copy.6.pairs
  0.8 0.0 copy-start
  0.8 1.4 copy-done
  2.2 0.0 copy-start.2
  2.2 1.6 copy-done.2
  3.8 9.0 %layer_one.1.src = f32[512,8,128]{2,1,0:T(8,128)S(1)} custom-call(s32[3,8,2]{2,1,0:T(8,128)S(1)} %copy.6.pairs, f32[3,2,256,256]{3,2,1,0:T(8,128)S(1)} %copy-done, f32[8,256,256]{2,1,0:T(8,128)S(1)} %bitcast.2), custom_call_target="tpu_custom_call" | custom-call | tf_op jit(solution)/shard_map/layer_one/pallas_call | solution.py:195
  12.7 0.0 copy-start.1
  12.7 77.7 %exchange.2.got = f32[512,8,128]{2,1,0:T(8,128)S(1)} custom-call(f32[512,8,128]{2,1,0:T(8,128)S(1)} %layer_one.1.src), custom_call_target="tpu_custom_call" | custom-call | tf_op jit(solution)/shard_map/exchange/pallas_call | solution.py:180
  90.4 0.0 copy-done.1
  90.4 13.4 %layer_two.1.src = f32[512,8,128]{2,1,0:T(8,128)S(1)} custom-call(s32[3,8,2]{2,1,0:T(8,128)S(1)} %copy.6.pairs, f32[3,2,256,256]{3,2,1,0:T(8,128)S(1)} %copy-done.1, f32[512,8,128]{2,1,0:T(8,128)S(1)} %exchange.2.got), custom_call_target="tpu_custom_call" | custom-call | tf_op jit(solution)/shard_map/layer_two/pallas_call | solution.py:199
  103.8 64.9 %exchange.3.got = f32[512,8,128]{2,1,0:T(8,128)S(1)} custom-call(f32[512,8,128]{2,1,0:T(8,128)S(1)} %layer_two.1.src), custom_call_target="tpu_custom_call" | custom-call | tf_op jit(solution)/shard_map/exchange/pallas_call | solution.py:180
  168.8 9.6 %layer_three.1 = f32[8,256,256]{2,1,0:T(8,128)} custom-call(s32[3,8,2]{2,1,0:T(8,128)S(1)} %copy.6.pairs, f32[3,2,256,256]{3,2,1,0:T(8,128)S(1)} %copy-done.1, f32[512,8,128]{2,1,0:T(8,128)S(1)} %exchange.3.got), custom_call_target="tpu_custom_call" | custom-call | tf_op jit(solution)/shard_map/layer_three/pallas_call | solution.py:201
Async XLA Ops:
  0.8 1.4 copy-start
  2.2 1.6 copy-start.2
  12.7 77.7 %copy-start.1 = (f32[3,2,256,256]{3,2,1,0:T(8,128)S(1)}, f32[3,2,256,256]{3,2,1,0:T(8,128)}, u32[]{:S(2)}) copy-start(f32[3,2,256,256]{3,2,1,0:T(8,128)} %gates.5) | copy-start | bytes 4718596

commit v2 on v0

v2 whole, which is shorter than its diff:
```python
import jax
import jax.numpy as jnp
from jax import lax
from jax.sharding import PartitionSpec as P
import jax.experimental.pallas as pl
import jax.experimental.pallas.tpu as pltpu

MESH = pl.DeviceIdType.MESH
GRPS, DEVS = 16, 32
NODES = GRPS * DEVS
HIGH, GATE = 8, 256
BLOCKS, BLOCK = 8, 64
NT = (((1,), (1,)), ((), ()))
NN = (((1,), (0,)), ((), ()))


def sign_of(flat, pairs, layer):
    parity = jnp.zeros_like(flat)
    for number in range(8):
        one = jnp.right_shift(flat, pairs[layer, 0, number])
        two = jnp.right_shift(flat, pairs[layer, 1, number])
        parity = parity ^ (one & two)
    return (1 - 2 * (parity & 1)).astype(jnp.float32)


def iota(shape, dim):
    return lax.broadcasted_iota(jnp.int32, shape, dim)


def split(values):
    high = values.astype(jnp.bfloat16)
    low = (values - high.astype(jnp.float32)).astype(jnp.bfloat16)
    return high, low


def split_gate(gate):
    high, low = split(gate)
    return jnp.concatenate([high, high, low], axis=1)


def by_last(state, last):
    high, low = split(state)
    wide = jnp.concatenate([high, low, high], axis=1)
    return lax.dot_general(wide, last, NT, preferred_element_type=jnp.float32)


def by_middle(middle, state):
    high, low = split(state)
    tall = jnp.concatenate([high, low, high], axis=0)
    return lax.dot_general(middle, tall, NN, preferred_element_type=jnp.float32)


def regroup(tiles):
    group = iota((8, 128), 1) // 16
    tiles = [pltpu.roll(t, 16 * q, 1) if q else t for q, t in enumerate(tiles)]
    for bit in range(3):
        chosen = (group // 2**bit) % 2 == 1
        tiles = [jnp.where(chosen, tiles[(v + 2**bit) % 8], tiles[v]) for v in range(8)]
    return [pltpu.roll(tiles[8 - p], 128 - 16 * p, 1) if p else tiles[0] for p in range(8)]


class Place:
    def __init__(self):
        self.grp, self.dev = lax.axis_index("grp"), lax.axis_index("dev")
        self.x, self.y = self.grp % 4, (self.grp // 4) * 2 + (self.dev // 2) % 2
        self.z, self.core = self.dev // 4, self.dev % 2
        self.me = self.grp * DEVS + self.dev

    def dev_of(self, block, step):
        z = (self.z + block // 4 + 2 * step) % 8
        low = (self.y + (block // 2) % 2) % 2
        return (z * 2 + low) * 2 + (self.core + block % 2) % 2

    def partner(self, block, step):
        mixed = (step * 27) % BLOCK
        x = (self.x + mixed % 4) % 4
        y = (self.y + (block // 2) % 2 + 2 * ((mixed // 4) % 4)) % 8
        z = (self.z + block // 4 + 2 * (mixed // 16)) % 8
        return (y // 2) * 4 + x, (z * 2 + y % 2) * 2 + (self.core + block % 2) % 2


def send_blocks(place, state, tiles, got, send_sem, recv_sem, sign=None):
    def block_body(block, carry):
        for step in range(4):
            dev = place.dev_of(block, step)
            rows = pl.ds(pl.multiple_of(dev * 8, 8), 8)
            for half in range(2):
                cols = pl.ds(half * 128, 128)
                out = regroup([state[h, rows, cols] for h in range(HIGH)])
                for p in range(8):
                    tile = out[p] if sign is None else out[p] * sign
                    tiles[(half * 8 + p) * DEVS + dev] = tile

        @pl.when(block == 0)
        def _():
            pltpu.make_async_copy(
                tiles.at[place.me], got.at[place.me], recv_sem.at[0]
            ).start()

        def send(step, inner):
            grp, dev = place.partner(block, step)
            pltpu.make_async_remote_copy(
                src_ref=tiles.at[grp * DEVS + dev],
                dst_ref=got.at[place.me],
                send_sem=send_sem,
                recv_sem=recv_sem.at[block],
                device_id=(grp, dev),
                device_id_type=MESH,
            ).start()
            return inner

        lax.fori_loop(jnp.where(block == 0, 1, 0), BLOCK, send, 0)
        return carry

    lax.fori_loop(0, BLOCKS, block_body, 0)


def take_blocks(place, got, staged, state, last, send_sem, recv_sem, sign=None):
    def block_body(block, carry):
        some = pl.ds(0, BLOCK)
        pltpu.make_async_remote_copy(
            src_ref=got.at[some],
            dst_ref=got.at[some],
            send_sem=send_sem,
            recv_sem=recv_sem.at[block],
            device_id=((place.grp + 1) % GRPS, place.dev),
            device_id_type=MESH,
        ).wait_recv()
        for step in range(4):
            dev = place.dev_of(block, step)
            for half in range(2):
                parts = [got[(half * 8 + p) * DEVS + dev] for p in range(8)]
                out = regroup(parts if sign is None else [part * sign for part in parts])
                for h in range(HIGH):
                    row = (step * HIGH + h) * 8
                    staged[row : row + 8, half * 128 : half * 128 + 128] = out[h]
        product = by_last(staged[...], last[...])
        for step in range(4):
            rows = pl.ds(pl.multiple_of(place.dev_of(block, step) * 8, 8), 8)
            for h in range(HIGH):
                row = (step * HIGH + h) * 8
                state[h, rows, :] = product[row : row + 8]
        return carry

    lax.fori_loop(0, BLOCKS, block_body, 0)


def window_kernel(
    pairs, gates, x, out,
    x_here, gates_here, wide, state, other, staged, row_sign,
    tiles_one, got_one, tiles_two, got_two,
    x_sem, gate_sem, out_sem, send_sem, recv_one, recv_two,
):
    place = Place()
    gate_copy = pltpu.make_async_copy(gates, gates_here, gate_sem)
    gate_copy.start()
    x_copies = [pltpu.make_async_copy(x.at[h], x_here.at[h], x_sem.at[h]) for h in range(HIGH)]
    for copy in x_copies:
        copy.start()

    barrier = pltpu.get_barrier_semaphore()

    def greet(step, carry):
        other_me = (place.me + step) % NODES
        pl.semaphore_signal(
            barrier, inc=1, device_id=(other_me // DEVS, other_me % DEVS), device_id_type=MESH
        )
        return carry

    lax.fori_loop(1, NODES, greet, 0)

    base = sign_of(iota((GATE, GATE), 0) * 256 + iota((GATE, GATE), 1), pairs, 0)
    rows = iota((GATE, 128), 0) * 256
    row_sign[...] = sign_of((iota((GATE, 128), 1) % 8) * 65536 + rows, pairs, 0) * sign_of(rows, pairs, 0)
    level = iota((8, GATE), 0) * 65536
    column = iota((8, GATE), 1)
    col_sign = (
        sign_of(level + column, pairs, 0) * sign_of(column, pairs, 0) * sign_of(level, pairs, 0)
    )

    gate_copy.wait()
    middle, last = split_gate(gates_here[0, 0]), split_gate(gates_here[0, 1])
    for h in range(HIGH):
        x_copies[h].wait()
        signed = x_here[h] * base * row_sign[:, h : h + 1] * col_sign[h : h + 1, :]
        state[h] = by_middle(middle, by_last(signed, last))

    pl.semaphore_wait(barrier, NODES - 1)
    send_blocks(place, state, tiles_one, got_one, send_sem.at[0], recv_one)

    for number, (layer, which) in enumerate(((1, 0), (1, 1), (2, 0), (2, 1))):
        wide[number] = split_gate(gates_here[layer, which])
    e, f = place.dev, place.grp
    lane = iota((8, 128), 1)
    flat = (lane // 16) * 65536 + (e * 8 + iota((8, 128), 0)) * 256 + f * 16 + lane % 16
    sign_one, sign_two = sign_of(flat, pairs, 1), sign_of(flat, pairs, 2)

    take_blocks(place, got_one, staged, other, wide.at[1], send_sem.at[0], recv_one, sign_one)
    for h in range(HIGH):
        state[h] = by_middle(wide[0], other[h])
    send_blocks(place, state, tiles_two, got_two, send_sem.at[1], recv_two, sign_two)
    take_blocks(place, got_two, staged, other, wide.at[3], send_sem.at[1], recv_two)
    out_copies = []
    for h in range(HIGH):
        x_here[h] = by_middle(wide[2], other[h])
        out_copies.append(pltpu.make_async_copy(x_here.at[h], out.at[h], out_sem.at[h]))
        out_copies[h].start()

    most = pl.ds(0, NODES - 1)
    for number, tiles in enumerate((tiles_one, tiles_two)):
        pltpu.make_async_remote_copy(
            src_ref=tiles.at[most],
            dst_ref=tiles.at[most],
            send_sem=send_sem.at[number],
            recv_sem=recv_one.at[0],
            device_id=((place.grp + 1) % GRPS, place.dev),
            device_id_type=MESH,
        ).wait_send()
    for copy in out_copies:
        copy.wait()


SMEM = pl.BlockSpec(memory_space=pltpu.SMEM)
ANY = pl.BlockSpec(memory_space=pl.ANY)
STATE = jax.ShapeDtypeStruct((HIGH, GATE, GATE), jnp.float32)


def per_device(amplitudes, joined_gates, pair_qubits):
    state = amplitudes.reshape(HIGH, GATE, GATE)
    held = pltpu.VMEM((HIGH, GATE, GATE), jnp.float32)
    tiles = pltpu.VMEM((NODES, 8, 128), jnp.float32)
    out = pl.pallas_call(
        window_kernel,
        out_shape=STATE,
        in_specs=[SMEM, ANY, ANY],
        out_specs=ANY,
        scratch_shapes=[
            held,
            pltpu.VMEM((3, 2, GATE, GATE), jnp.float32),
            pltpu.VMEM((4, GATE, 3 * GATE), jnp.bfloat16),
            held,
            held,
            pltpu.VMEM((GATE, GATE), jnp.float32),
            pltpu.VMEM((GATE, 128), jnp.float32),
            tiles,
            tiles,
            tiles,
            tiles,
            pltpu.SemaphoreType.DMA((HIGH,)),
            pltpu.SemaphoreType.DMA,
            pltpu.SemaphoreType.DMA((HIGH,)),
            pltpu.SemaphoreType.DMA((2,)),
            pltpu.SemaphoreType.DMA((BLOCKS,)),
            pltpu.SemaphoreType.DMA((BLOCKS,)),
        ],
        name="window",
        compiler_params=pltpu.CompilerParams(
            collective_id=0, has_side_effects=True, vmem_limit_bytes=56 * 2**20
        ),
        cost_estimate=pl.CostEstimate(flops=5 * 2**29, bytes_accessed=2**23, transcendentals=0),
    )(pair_qubits.transpose(0, 2, 1), joined_gates, state)
    return out.reshape(amplitudes.shape)


def solution(mesh):
    placed = (P("grp", "dev", None, None, None), P(), P())
    return jax.shard_map(
        per_device,
        mesh=mesh,
        in_specs=placed,
        out_specs=P("grp", "dev", None, None, None),
        check_vma=False,
    )
```

time: 319 us -> 140 us (0.44)
  blocking collectives: 188 us -> 0 us
  Pallas kernels: 0 us -> 136 us
  matrix products: 63.1 us -> 0 us
  waiting for transfers between devices: 38.5 us -> 0 us
  local copies, waits for them, and re-layouts: 19.2 us -> 3.05 us
  starting transfers between devices: 8.49 us -> 0 us
    all_to_all x3 -> x0, blocking collectives: 188 us -> none  [the longest x2 148 us: swap_devices(): lax.all_to_all(current, 'dev', split_axis=3, concat_axis=3, tiled=True)]
    pallas_call x0 -> x1, Pallas kernels: none -> 136 us  [per_device(): pl.pallas_call(window_kernel, out_shape=STATE, in_specs=[SMEM, ANY, ANY],...]
    dot_general x6 -> x0, matrix products: 63.1 us -> none  [the longest x3 37.9 us: along_last(): jnp.einsum('jk,xyhik->xyhij', matrix, current, precision=lax.Precision.HI...]
    all_to_all x1 -> x0, waiting for transfers between devices: 38.5 us -> none  [swap_groups(): lax.all_to_all(current, 'grp', split_axis=4, concat_axis=4, tiled=True)]
    all_to_all x1 -> x0, starting transfers between devices: 8.49 us -> none  [swap_groups(): lax.all_to_all(current, 'grp', split_axis=4, concat_axis=4, tiled=True)]
    all_to_all x4 -> x0, local copies, waits for them, and re-layouts: 7.38 us -> none  [the longest x2 3.75 us: swap_groups(): lax.all_to_all(current, 'grp', split_axis=4, concat_axis=4, tiled=True)]
    transpose x2 -> x0, local copies, waits for them, and re-layouts: 4.35 us -> none  [along_middle(): jnp.einsum('ik,xyhkj->xyhij', matrix, current, precision=lax.Precision.HI...]
    mul x2 -> x0, local copies, waits for them, and re-layouts: 3.42 us -> none  [apply_signs(): return current * sign_of(flat_index, pair_row)[None, None]]
  transfers between devices with their start and end apart: 1 -> 0, of which waited for: 1 -> 0; matrix products, arithmetic and copies ran while one was open for 0% -> 0% of each run, Pallas kernels for 0% -> 0%
where the time goes in v2:
time: 140 us; the launch traced here: 139 us
  Pallas kernels  136 us (97%)
  local copies, waits for them, and re-layouts  3.05 us (2%)
    pallas_call x1, Pallas kernels, per_device(): pl.pallas_call(window_kernel, out_shape=STATE, in_specs=[SMEM, ANY, ANY],...  136 us
    unnamed x1, local copies, waits for them, and re-layouts  3.05 us

profile of v2, /device:TPU:1, one launch (start us, length us, event | category | flops | bytes accessed | tf_op | source)
XLA Modules:
  0.0 139.4 jit_solution(16583914583174552890)
XLA Ops:
  0.0 136.3 %window.1 = f32[8,256,256]{2,1,0:T(8,128)} custom-call(s32[3,2,8]{2,1,0:T(2,128)} %bitcast.5, f32[3,2,256,256]{3,2,1,0:T(8,128)} %gates.1, f32[8,256,256]{2,1,0:T(8,128)} %bitcast.4), custom_call_target="tpu_custom_call" | custom-call | flops 2684354560 | bytes 8388608 | tf_op jit(solution)/shard_map/window/pallas_call | solution.py:232
  136.4 3.0 %copy.5 = f32[1,1,8,256,256]{4,3,2,1,0:T(8,128)} copy(f32[1,1,8,256,256]{4,3,2,1,0:T(8,128)} %bitcast.3) | data formatting | bytes 4194304

commit v3 on v2

--- a/solution.py
+++ b/solution.py
@@ -67,9 +67,15 @@
         self.me = self.grp * DEVS + self.dev
 
     def dev_of(self, block, step):
-        z = (self.z + block // 4 + 2 * step) % 8
-        low = (self.y + (block // 2) % 2) % 2
-        return (z * 2 + low) * 2 + (self.core + block % 2) % 2
+        odd, low, core = self.origin(block)
+        return ((odd + 2 * step) * 2 + low) * 2 + core
+
+    def origin(self, block):
+        return (
+            (self.z + block // 4) % 2,
+            (self.y + (block // 2) % 2) % 2,
+            (self.core + block % 2) % 2,
+        )
 
     def partner(self, block, step):
         mixed = (step * 27) % BLOCK
@@ -115,7 +121,7 @@
     lax.fori_loop(0, BLOCKS, block_body, 0)
 
 
-def take_blocks(place, got, staged, state, last, send_sem, recv_sem, sign=None):
+def take_blocks(place, got, staged, state, last, send_sem, recv_sem, sign=None, done=None, done_sem=None):
     def block_body(block, carry):
         some = pl.ds(0, BLOCK)
         pltpu.make_async_remote_copy(
@@ -135,6 +141,12 @@
                     row = (step * HIGH + h) * 8
                     staged[row : row + 8, half * 128 : half * 128 + 128] = out[h]
         product = by_last(staged[...], last[...])
+        if done is not None:
+            odd, low, core = place.origin(block)
+            number = (odd * 2 + low) * 2 + core
+            state[number] = product
+            pltpu.make_async_copy(state.at[number], done.at[number], done_sem).start()
+            return carry
         for step in range(4):
             rows = pl.ds(pl.multiple_of(place.dev_of(block, step) * 8, 8), 8)
             for h in range(HIGH):
@@ -146,10 +158,10 @@
 
 
 def window_kernel(
-    pairs, gates, x, out,
+    pairs, gates, x, half_done,
     x_here, gates_here, wide, state, other, staged, row_sign,
     tiles_one, got_one, tiles_two, got_two,
-    x_sem, gate_sem, out_sem, send_sem, recv_one, recv_two,
+    x_sem, gate_sem, out_sem, send_sem, recv_one, recv_two, ready,
 ):
     place = Place()
     gate_copy = pltpu.make_async_copy(gates, gates_here, gate_sem)
@@ -160,14 +172,23 @@
 
     barrier = pltpu.get_barrier_semaphore()
 
-    def greet(step, carry):
-        other_me = (place.me + step) % NODES
-        pl.semaphore_signal(
-            barrier, inc=1, device_id=(other_me // DEVS, other_me % DEVS), device_id_type=MESH
-        )
-        return carry
-
-    lax.fori_loop(1, NODES, greet, 0)
+    def greet_dev(step, carry):
+        dev = (place.dev + step) % DEVS
+        pl.semaphore_signal(barrier, inc=1, device_id=(place.grp, dev), device_id_type=MESH)
+        return carry
+
+    def greet_grp(step, carry):
+        grp = (place.grp + step) % GRPS
+        pl.semaphore_signal(barrier, inc=1, device_id=(grp, place.dev), device_id_type=MESH)
+        return carry
+
+    def say_ready(step, carry):
+        grp = (place.grp + step) % GRPS
+        pl.semaphore_signal(ready, inc=1, device_id=(grp, place.dev), device_id_type=MESH)
+        return carry
+
+    lax.fori_loop(1, DEVS, greet_dev, 0)
+    lax.fori_loop(1, GRPS, greet_grp, 0)
 
     base = sign_of(iota((GATE, GATE), 0) * 256 + iota((GATE, GATE), 1), pairs, 0)
     rows = iota((GATE, 128), 0) * 256
@@ -181,14 +202,17 @@
     gate_copy.wait()
     middle, last = split_gate(gates_here[0, 0]), split_gate(gates_here[0, 1])
     for h in range(HIGH):
+        if h == 4:
+            pl.semaphore_wait(barrier, DEVS + GRPS - 2)
+            lax.fori_loop(1, GRPS, say_ready, 0)
         x_copies[h].wait()
         signed = x_here[h] * base * row_sign[:, h : h + 1] * col_sign[h : h + 1, :]
         state[h] = by_middle(middle, by_last(signed, last))
 
-    pl.semaphore_wait(barrier, NODES - 1)
+    pl.semaphore_wait(ready, GRPS - 1)
     send_blocks(place, state, tiles_one, got_one, send_sem.at[0], recv_one)
 
-    for number, (layer, which) in enumerate(((1, 0), (1, 1), (2, 0), (2, 1))):
+    for number, (layer, which) in enumerate(((1, 0), (1, 1), (2, 1))):
         wide[number] = split_gate(gates_here[layer, which])
     e, f = place.dev, place.grp
     lane = iota((8, 128), 1)
@@ -199,12 +223,9 @@
     for h in range(HIGH):
         state[h] = by_middle(wide[0], other[h])
     send_blocks(place, state, tiles_two, got_two, send_sem.at[1], recv_two, sign_two)
-    take_blocks(place, got_two, staged, other, wide.at[3], send_sem.at[1], recv_two)
-    out_copies = []
-    for h in range(HIGH):
-        x_here[h] = by_middle(wide[2], other[h])
-        out_copies.append(pltpu.make_async_copy(x_here.at[h], out.at[h], out_sem.at[h]))
-        out_copies[h].start()
+    take_blocks(
+        place, got_two, staged, other, wide.at[2], send_sem.at[1], recv_two, None, half_done, out_sem
+    )
 
     most = pl.ds(0, NODES - 1)
     for number, tiles in enumerate((tiles_one, tiles_two)):
@@ -216,7 +237,28 @@
             device_id=((place.grp + 1) % GRPS, place.dev),
             device_id_type=MESH,
         ).wait_send()
-    for copy in out_copies:
+    pltpu.make_async_copy(other, half_done, out_sem).wait()
+
+
+def last_kernel(half_done, gates, out, half_here, gate_here, out_here, gate_sem, in_sem, out_sem):
+    gate_copy = pltpu.make_async_copy(gates.at[2, 0], gate_here, gate_sem)
+    gate_copy.start()
+    half_copy = pltpu.make_async_copy(half_done, half_here, in_sem)
+    half_copy.start()
+    gate_copy.wait()
+    middle = split_gate(gate_here[...])
+    half_copy.wait()
+    copies = []
+    for h in range(HIGH):
+        parts = []
+        for dev in range(DEVS):
+            z, low = dev // 4, dev % 4
+            row = ((z // 2) * HIGH + h) * 8
+            parts.append(half_here[(z % 2) * 4 + low, row : row + 8, :])
+        out_here[h] = by_middle(middle, jnp.concatenate(parts, axis=0))
+        copies.append(pltpu.make_async_copy(out_here.at[h], out.at[h], out_sem.at[h]))
+        copies[h].start()
+    for copy in copies:
         copy.wait()
 
 
@@ -229,7 +271,7 @@
     state = amplitudes.reshape(HIGH, GATE, GATE)
     held = pltpu.VMEM((HIGH, GATE, GATE), jnp.float32)
     tiles = pltpu.VMEM((NODES, 8, 128), jnp.float32)
-    out = pl.pallas_call(
+    half_done = pl.pallas_call(
         window_kernel,
         out_shape=STATE,
         in_specs=[SMEM, ANY, ANY],
@@ -237,7 +279,7 @@
         scratch_shapes=[
             held,
             pltpu.VMEM((3, 2, GATE, GATE), jnp.float32),
-            pltpu.VMEM((4, GATE, 3 * GATE), jnp.bfloat16),
+            pltpu.VMEM((3, GATE, 3 * GATE), jnp.bfloat16),
             held,
             held,
             pltpu.VMEM((GATE, GATE), jnp.float32),
@@ -248,10 +290,11 @@
             tiles,
             pltpu.SemaphoreType.DMA((HIGH,)),
             pltpu.SemaphoreType.DMA,
-            pltpu.SemaphoreType.DMA((HIGH,)),
+            pltpu.SemaphoreType.DMA,
             pltpu.SemaphoreType.DMA((2,)),
             pltpu.SemaphoreType.DMA((BLOCKS,)),
             pltpu.SemaphoreType.DMA((BLOCKS,)),
+            pltpu.SemaphoreType.REGULAR,
         ],
         name="window",
         compiler_params=pltpu.CompilerParams(
@@ -259,6 +302,22 @@
         ),
         cost_estimate=pl.CostEstimate(flops=5 * 2**29, bytes_accessed=2**23, transcendentals=0),
     )(pair_qubits.transpose(0, 2, 1), joined_gates, state)
+    out = pl.pallas_call(
+        last_kernel,
+        out_shape=STATE,
+        in_specs=[ANY, ANY],
+        out_specs=ANY,
+        scratch_shapes=[
+            held,
+            pltpu.VMEM((GATE, GATE), jnp.float32),
+            held,
+            pltpu.SemaphoreType.DMA,
+            pltpu.SemaphoreType.DMA,
+            pltpu.SemaphoreType.DMA((HIGH,)),
+        ],
+        name="last_product",
+        compiler_params=pltpu.CompilerParams(vmem_limit_bytes=56 * 2**20),
+    )(half_done, joined_gates)
     return out.reshape(amplitudes.shape)
 
 

time: 140 us -> 130 us (0.929)
  Pallas kernels: 136 us -> 130 us
  local copies, waits for them, and re-layouts: 3.05 us -> 0 us
    pallas_call x1, Pallas kernels: 136 us -> 126 us  [per_device(): pl.pallas_call(window_kernel, out_shape=STATE, in_specs=[SMEM, ANY, ANY],...]
    pallas_call x0 -> x1, Pallas kernels: none -> 3.6 us  [per_device(): pl.pallas_call(last_kernel, out_shape=STATE, in_specs=[ANY, ANY], out_spe...]
    unnamed x1 -> x0, local copies, waits for them, and re-layouts: 3.05 us -> none
where the time goes in v3:
time: 130 us
  Pallas kernels  130 us (100%)
    pallas_call x1, Pallas kernels, per_device(): pl.pallas_call(window_kernel, out_shape=STATE, in_specs=[SMEM, ANY, ANY],...  126 us
    pallas_call x1, Pallas kernels, per_device(): pl.pallas_call(last_kernel, out_shape=STATE, in_specs=[ANY, ANY], out_spe...  3.6 us

profile of v3, /device:TPU:1, one launch (start us, length us, event | category | flops | bytes accessed | tf_op | source)
XLA Modules:
  0.0 129.7 jit_solution(8662873596531475977)
XLA Ops:
  0.0 126.1 %window.1.half_done = f32[8,256,256]{2,1,0:T(8,128)} custom-call(s32[3,2,8]{2,1,0:T(2,128)} %bitcast.4, f32[3,2,256,256]{3,2,1,0:T(8,128)} %gates.3, f32[8,256,256]{2,1,0:T(8,128)} %bitcast.3), custom_call_target="tpu_custom_call" | custom-call | flops 2684354560 | bytes 8388608 | tf_op jit(solution)/shard_map/window/pallas_call | solution.py:274
  126.1 3.6 %last_product.1 = f32[8,256,256]{2,1,0:T(8,128)} custom-call(f32[8,256,256]{2,1,0:T(8,128)} %window.1.half_done, f32[3,2,256,256]{3,2,1,0:T(8,128)} %gates.3), custom_call_target="tpu_custom_call" | custom-call | tf_op jit(solution)/shard_map/last_product/pallas_call | solution.py:305

commit v4 on v2

v4 whole, which is shorter than its diff:
```python
import jax
import jax.numpy as jnp
from jax import lax
from jax.sharding import PartitionSpec as P
import jax.experimental.pallas as pl
import jax.experimental.pallas.tpu as pltpu

MESH = pl.DeviceIdType.MESH
GRPS, DEVS, PAIRED = 16, 32, 16
CHIPS = GRPS * PAIRED
HIGH, HALF, GATE = 8, 4, 256
BLOCKS, BLOCK = 4, 64
NT = (((1,), (1,)), ((), ()))
NN = (((1,), (0,)), ((), ()))


def sign_of(flat, pairs, layer):
    parity = jnp.zeros_like(flat)
    for number in range(8):
        one = jnp.right_shift(flat, pairs[layer, 0, number])
        two = jnp.right_shift(flat, pairs[layer, 1, number])
        parity = parity ^ (one & two)
    return (1 - 2 * (parity & 1)).astype(jnp.float32)


def iota(shape, dim):
    return lax.broadcasted_iota(jnp.int32, shape, dim)


def split(values):
    high = values.astype(jnp.bfloat16)
    low = (values - high.astype(jnp.float32)).astype(jnp.bfloat16)
    return high, low


def split_gate(gate):
    high, low = split(gate)
    return jnp.concatenate([high, high, low], axis=1)


def by_last(state, last):
    high, low = split(state)
    wide = jnp.concatenate([high, low, high], axis=1)
    return lax.dot_general(wide, last, NT, preferred_element_type=jnp.float32)


def by_middle(middle, state):
    high, low = split(state)
    tall = jnp.concatenate([high, low, high], axis=0)
    return lax.dot_general(middle, tall, NN, preferred_element_type=jnp.float32)


def regroup(tiles):
    group = iota((8, 128), 1) // 16
    tiles = [pltpu.roll(t, 16 * q, 1) if q else t for q, t in enumerate(tiles)]
    for bit in range(3):
        chosen = (group // 2**bit) % 2 == 1
        tiles = [jnp.where(chosen, tiles[(v + 2**bit) % 8], tiles[v]) for v in range(8)]
    return [pltpu.roll(tiles[8 - p], 128 - 16 * p, 1) if p else tiles[0] for p in range(8)]


def pick(index, values):
    chosen = values[3]
    for number in (2, 1, 0):
        chosen = jnp.where(index == number, values[number], chosen)
    return chosen


class Place:
    def __init__(self):
        self.grp, self.dev = lax.axis_index("grp"), lax.axis_index("dev")
        self.x, self.y = self.grp % 4, (self.grp // 4) * 2 + (self.dev // 2) % 2
        self.z, self.core = self.dev // 4, self.dev % 2
        self.chip = self.grp * PAIRED + self.dev // 2
        self.sibling = (self.dev // 2) * 2 + 1 - self.core

    def paired(self, block, step):
        return ((self.z + block // 2) % 2 + 2 * step) * 2 + (self.y + block % 2) % 2

    def at(self, dx, dy, dz):
        x, y, z = (self.x + dx) % 4, (self.y + dy) % 8, (self.z + dz) % 8
        return (y // 2) * 4 + x, z * 2 + y % 2

    def partner(self, block, step, near_last):
        odd_z, odd_y = block // 2, block % 2
        mixed = (step * 27) % BLOCK
        dx, dy, dz = mixed % 4, 2 * ((mixed // 4) % 4), 2 * (mixed // 16)
        if near_last:
            far = (4, 2, 6, 0)
            last = block == 0
            dx = jnp.where(last, pick(step % 4, (2, 1, 3, 0)), dx)
            dy = jnp.where(last, pick((step // 4) % 4, far), dy)
            dz = jnp.where(last, pick(step // 16, far), dz)
        return self.at(dx, dy + odd_y, dz + odd_z)


def pack_block(place, half, block, state, tiles, sign=None):
    for step in range(4):
        paired = place.paired(block, step)
        for side in range(2):
            cols = pl.ds(side * 128, 128)
            parts = []
            for other in range(2):
                dev = paired * 2 + (place.core + other) % 2
                rows = pl.ds(pl.multiple_of(dev * 8, 8), 8)
                parts += [state[half * HALF + h, rows, cols] for h in range(HALF)]
            out = regroup(parts)
            for p in range(8):
                tile = out[p] if sign is None else out[p] * sign
                tiles[half, (side * 8 + p) * PAIRED + paired] = tile


def send_block(place, half, block, tiles, got, send_sem, recv_sem):
    def send(step, inner):
        grp, paired = place.partner(block, step, half == 1)
        chip = grp * PAIRED + paired

        @pl.when(chip != place.chip)
        def _():
            pltpu.make_async_remote_copy(
                src_ref=tiles.at[half, chip],
                dst_ref=got.at[half, place.chip],
                send_sem=send_sem,
                recv_sem=recv_sem.at[half * BLOCKS + block],
                device_id=(grp, paired * 2 + place.core),
                device_id_type=MESH,
            ).start()

        return inner

    lax.fori_loop(0, BLOCK, send, 0)


def keep_own(place, half, tiles, got, recv_sem):
    pltpu.make_async_copy(
        tiles.at[half, place.chip], got.at[half, place.chip], recv_sem.at[half * BLOCKS]
    ).start()


def send_half(place, half, state, tiles, got, send_sem, recv_sem, sign=None):
    def block_body(number, carry):
        block = BLOCKS - 1 - number
        pack_block(place, half, block, state, tiles, sign)
        send_block(place, half, block, tiles, got, send_sem, recv_sem)
        return carry

    lax.fori_loop(0, BLOCKS, block_body, 0)
    keep_own(place, half, tiles, got, recv_sem)


def take_half(
    place, half, got, state, last, mine, away, come, recv_sem, away_sem, come_sem, sign=None
):
    def keep(rows, block, core):
        product = by_last(rows, last[...])
        for step in range(4):
            dev = place.paired(block, step) * 2 + core
            where = pl.ds(pl.multiple_of(dev * 8, 8), 8)
            for h in range(HALF):
                row = (step * HALF + h) * 8
                state[half * HALF + h, where, :] = product[row : row + 8]

    def forward(block):
        slot = half * BLOCKS + block
        return pltpu.make_async_remote_copy(
            src_ref=away.at[slot],
            dst_ref=come.at[slot],
            send_sem=away_sem,
            recv_sem=come_sem.at[slot],
            device_id=(place.grp, place.sibling),
            device_id_type=MESH,
        )

    def keep_come(block):
        forward(block).wait_recv()
        keep(come[half * BLOCKS + block], block, 1 - place.core)

    def block_body(number, carry):
        block = BLOCKS - 1 - number
        slot = half * BLOCKS + block
        some = pl.ds(0, BLOCK)
        pltpu.make_async_copy(got.at[half, some], got.at[half, some], recv_sem.at[slot]).wait()
        for step in range(4):
            paired = place.paired(block, step)
            for side in range(2):
                cols = pl.ds(side * 128, 128)
                parts = [got[half, (side * 8 + p) * PAIRED + paired] for p in range(8)]
                out = regroup(parts if sign is None else [part * sign for part in parts])
                for h in range(HALF):
                    rows = pl.ds((step * HALF + h) * 8, 8)
                    mine[rows, cols] = out[h]
                    away[slot, rows, cols] = out[HALF + h]
        forward(block).start()
        keep(mine[...], block, place.core)

        @pl.when(number > 0)
        def _():
            keep_come(block + 1)

        return carry

    lax.fori_loop(0, BLOCKS, block_body, 0)
    keep_come(0)


def window_kernel(
    pairs, gates, x, half_done,
    x_here, gates_here, wide, state, other, mine, row_sign,
    tiles_one, got_one, tiles_two, got_two, away_one, come_one, away_two, come_two,
    x_sem, gate_sem, out_sem, send_sem, recv_one, recv_two, away_sem, come_sem_one, come_sem_two, ready,
):
    place = Place()

    barrier = pltpu.get_barrier_semaphore()

    def greet_plane(step, carry):
        grp, paired = place.at(step % 4, step // 4, 0)
        pl.semaphore_signal(
            barrier, inc=1, device_id=(grp, paired * 2 + place.core), device_id_type=MESH
        )
        return carry

    def tell_line(semaphore):
        def body(step, carry):
            grp, paired = place.at(0, 0, step)
            pl.semaphore_signal(
                semaphore, inc=1, device_id=(grp, paired * 2 + place.core), device_id_type=MESH
            )
            return carry

        lax.fori_loop(1, 8, body, 0)

    lax.fori_loop(1, 32, greet_plane, 0)
    tell_line(barrier)
    pl.semaphore_signal(
        barrier, inc=1, device_id=(place.grp, place.sibling), device_id_type=MESH
    )

    gate_copy = pltpu.make_async_copy(gates, gates_here, gate_sem)
    gate_copy.start()
    halves = [pl.ds(half * HALF, HALF) for half in range(2)]
    x_copies = [
        pltpu.make_async_copy(x.at[levels], x_here.at[levels], x_sem.at[half])
        for half, levels in enumerate(halves)
    ]
    for copy in x_copies:
        copy.start()

    base = sign_of(iota((GATE, GATE), 0) * 256 + iota((GATE, GATE), 1), pairs, 0)
    rows = iota((GATE, 128), 0) * 256
    row_sign[...] = sign_of((iota((GATE, 128), 1) % 8) * 65536 + rows, pairs, 0) * sign_of(rows, pairs, 0)
    level = iota((8, GATE), 0) * 65536
    column = iota((8, GATE), 1)
    col_sign = (
        sign_of(level + column, pairs, 0) * sign_of(column, pairs, 0) * sign_of(level, pairs, 0)
    )

    gate_copy.wait()
    middle, last = split_gate(gates_here[0, 0]), split_gate(gates_here[0, 1])

    def layer_one(half):
        x_copies[half].wait()
        for h in range(half * HALF, half * HALF + HALF):
            signed = x_here[h] * base * row_sign[:, h : h + 1] * col_sign[h : h + 1, :]
            state[h] = by_middle(middle, by_last(signed, last))

    def pack_body(block, carry):
        pack_block(place, 0, block, state, tiles_one)
        return carry

    def send_body(number, carry):
        send_block(place, 0, BLOCKS - 1 - number, tiles_one, got_one, send_sem.at[0], recv_one)
        return carry

    layer_one(0)
    pl.semaphore_wait(barrier, 31 + 7 + 1)
    tell_line(ready)
    lax.fori_loop(0, BLOCKS, pack_body, 0)
    layer_one(1)
    pl.semaphore_wait(ready, 7)
    lax.fori_loop(0, BLOCKS, send_body, 0)
    keep_own(place, 0, tiles_one, got_one, recv_one)
    send_half(place, 1, state, tiles_one, got_one, send_sem.at[0], recv_one)

    for number, (layer, which) in enumerate(((1, 0), (1, 1), (2, 0), (2, 1))):
        wide[number] = split_gate(gates_here[layer, which])
    lane = iota((8, 128), 1)
    levels, row = (lane // 16) % 4 * 65536, iota((8, 128), 0)
    column = place.grp * 16 + lane % 16
    both = (place.dev // 2) * 2 + (place.core + lane // 64) % 2
    arrives = levels + (both * 8 + row) * 256 + column
    leaves = levels + (place.dev * 8 + row) * 256 + column
    sign_one = [sign_of(arrives + half * HALF * 65536, pairs, 1) for half in range(2)]
    sign_two = [sign_of(leaves + half * HALF * 65536, pairs, 2) for half in range(2)]

    for half in range(2):
        take_half(
            place, half, got_one, other, wide.at[1], mine, away_one, come_one,
            recv_one, away_sem.at[0], come_sem_one, sign_one[half],
        )
        for h in range(half * HALF, half * HALF + HALF):
            state[h] = by_middle(wide[0], other[h])
        send_half(
            place, half, state, tiles_two, got_two, send_sem.at[1], recv_two, sign_two[half]
        )
    out_copies = []
    for half in range(2):
        take_half(
            place, half, got_two, other, wide.at[3], mine, away_two, come_two,
            recv_two, away_sem.at[1], come_sem_two,
        )
        source = other
        if half == 0:
            source = x_here
            for h in range(HALF):
                x_here[h] = by_middle(wide[2], other[h])
        out_copies.append(
            pltpu.make_async_copy(
                source.at[halves[half]], half_done.at[halves[half]], out_sem.at[half]
            )
        )
        out_copies[half].start()

    most = pl.ds(0, CHIPS - 1)
    for number, (tiles, away) in enumerate(((tiles_one, away_one), (tiles_two, away_two))):
        for half in range(2):
            part = tiles.at[half, most]
            pltpu.make_async_copy(part, part, send_sem.at[number]).wait()
        pltpu.make_async_copy(away, away, away_sem.at[number]).wait()
    for copy in out_copies:
        copy.wait()


def last_kernel(half_done, gates, out, half_here, gate_here, out_here, gate_sem, in_sem, out_sem):
    gate_copy = pltpu.make_async_copy(gates.at[2, 0], gate_here, gate_sem)
    gate_copy.start()
    copies = []
    for half in (1, 0):
        levels = pl.ds(half * HALF, HALF)
        copies.append(
            pltpu.make_async_copy(half_done.at[levels], half_here.at[levels], in_sem.at[half])
        )
        copies[-1].start()
    gate_copy.wait()
    middle = split_gate(gate_here[...])
    for copy in copies:
        copy.wait()
    finished = pl.ds(0, HALF)
    copies = [pltpu.make_async_copy(half_here.at[finished], out.at[finished], out_sem.at[0])]
    copies[0].start()
    for h in range(HALF):
        out_here[h] = by_middle(middle, half_here[HALF + h])
        copies.append(
            pltpu.make_async_copy(out_here.at[h], out.at[HALF + h], out_sem.at[1 + h])
        )
        copies[-1].start()
    for copy in copies:
        copy.wait()


SMEM = pl.BlockSpec(memory_space=pltpu.SMEM)
ANY = pl.BlockSpec(memory_space=pl.ANY)
STATE = jax.ShapeDtypeStruct((HIGH, GATE, GATE), jnp.float32)


def per_device(amplitudes, joined_gates, pair_qubits):
    state = amplitudes.reshape(HIGH, GATE, GATE)
    held = pltpu.VMEM((HIGH, GATE, GATE), jnp.float32)
    tiles = pltpu.VMEM((2, CHIPS, 8, 128), jnp.float32)
    within = pltpu.VMEM((2 * BLOCKS, 128, GATE), jnp.float32)
    dma = pltpu.SemaphoreType.DMA
    half_done = pl.pallas_call(
        window_kernel,
        out_shape=STATE,
        in_specs=[SMEM, ANY, ANY],
        out_specs=ANY,
        scratch_shapes=[
            held,
            pltpu.VMEM((3, 2, GATE, GATE), jnp.float32),
            pltpu.VMEM((4, GATE, 3 * GATE), jnp.bfloat16),
            held,
            held,
            pltpu.VMEM((128, GATE), jnp.float32),
            pltpu.VMEM((GATE, 128), jnp.float32),
            tiles,
            tiles,
            tiles,
            tiles,
            within,
            within,
            within,
            within,
            dma((2,)),
            dma,
            dma((2,)),
            dma((2,)),
            dma((2 * BLOCKS,)),
            dma((2 * BLOCKS,)),
            dma((2,)),
            dma((2 * BLOCKS,)),
            dma((2 * BLOCKS,)),
            pltpu.SemaphoreType.REGULAR,
        ],
        name="window",
        compiler_params=pltpu.CompilerParams(
            collective_id=0, has_side_effects=True, vmem_limit_bytes=56 * 2**20
        ),
        cost_estimate=pl.CostEstimate(flops=5 * 2**29, bytes_accessed=2**23, transcendentals=0),
    )(pair_qubits.transpose(0, 2, 1), joined_gates, state)
    out = pl.pallas_call(
        last_kernel,
        out_shape=STATE,
        in_specs=[ANY, ANY],
        out_specs=ANY,
        scratch_shapes=[
            held,
            pltpu.VMEM((GATE, GATE), jnp.float32),
            pltpu.VMEM((HALF, GATE, GATE), jnp.float32),
            dma,
            dma((2,)),
            dma((1 + HALF,)),
        ],
        name="last_product",
        compiler_params=pltpu.CompilerParams(vmem_limit_bytes=56 * 2**20),
    )(half_done, joined_gates)
    return out.reshape(amplitudes.shape)


def solution(mesh):
    placed = (P("grp", "dev", None, None, None), P(), P())
    return jax.shard_map(
        per_device,
        mesh=mesh,
        in_specs=placed,
        out_specs=P("grp", "dev", None, None, None),
        check_vma=False,
    )
```

time: 140 us -> 122 us (0.87)
  Pallas kernels: 136 us -> 122 us
  local copies, waits for them, and re-layouts: 3.05 us -> 0 us
    pallas_call x1, Pallas kernels: 136 us -> 119 us  [per_device(): pl.pallas_call(window_kernel, out_shape=STATE, in_specs=[SMEM, ANY, ANY],...]
    pallas_call x0 -> x1, Pallas kernels: none -> 3.06 us  [per_device(): pl.pallas_call(last_kernel, out_shape=STATE, in_specs=[ANY, ANY], out_spe...]
    unnamed x1 -> x0, local copies, waits for them, and re-layouts: 3.05 us -> none
where the time goes in v4:
time: 122 us
  Pallas kernels  122 us (100%)
    pallas_call x1, Pallas kernels, per_device(): pl.pallas_call(window_kernel, out_shape=STATE, in_specs=[SMEM, ANY, ANY],...  119 us
    pallas_call x1, Pallas kernels, per_device(): pl.pallas_call(last_kernel, out_shape=STATE, in_specs=[ANY, ANY], out_spe...  3.06 us

profile of v4, /device:TPU:1, one launch (start us, length us, event | category | flops | bytes accessed | tf_op | source)
XLA Modules:
  0.0 121.8 jit_solution(8541365522629551928)
XLA Ops:
  0.0 118.7 %window.1.half_done = f32[8,256,256]{2,1,0:T(8,128)} custom-call(s32[3,2,8]{2,1,0:T(2,128)} %bitcast.4, f32[3,2,256,256]{3,2,1,0:T(8,128)} %gates.3, f32[8,256,256]{2,1,0:T(8,128)} %bitcast.3), custom_call_target="tpu_custom_call" | custom-call | flops 2684354560 | bytes 8388608 | tf_op jit(solution)/shard_map/window/pallas_call | solution.py:372
  118.7 3.1 %last_product.1 = f32[8,256,256]{2,1,0:T(8,128)} custom-call(f32[8,256,256]{2,1,0:T(8,128)} %window.1.half_done, f32[3,2,256,256]{3,2,1,0:T(8,128)} %gates.3), custom_call_target="tpu_custom_call" | custom-call | tf_op jit(solution)/shard_map/last_product/pallas_call | solution.py:410

commit v5 on v4

--- a/solution.py
+++ b/solution.py
@@ -110,21 +110,24 @@
                 tiles[half, (side * 8 + p) * PAIRED + paired] = tile
 
 
+def send_one(place, half, block, grp, paired, tiles, got, send_sem, recv_sem):
+    pltpu.make_async_remote_copy(
+        src_ref=tiles.at[half, grp * PAIRED + paired],
+        dst_ref=got.at[half, place.chip],
+        send_sem=send_sem,
+        recv_sem=recv_sem.at[half * BLOCKS + block],
+        device_id=(grp, paired * 2 + place.core),
+        device_id_type=MESH,
+    ).start()
+
+
 def send_block(place, half, block, tiles, got, send_sem, recv_sem):
     def send(step, inner):
         grp, paired = place.partner(block, step, half == 1)
-        chip = grp * PAIRED + paired
-
-        @pl.when(chip != place.chip)
+
+        @pl.when(grp * PAIRED + paired != place.chip)
         def _():
-            pltpu.make_async_remote_copy(
-                src_ref=tiles.at[half, chip],
-                dst_ref=got.at[half, place.chip],
-                send_sem=send_sem,
-                recv_sem=recv_sem.at[half * BLOCKS + block],
-                device_id=(grp, paired * 2 + place.core),
-                device_id_type=MESH,
-            ).start()
+            send_one(place, half, block, grp, paired, tiles, got, send_sem, recv_sem)
 
         return inner
 
@@ -149,7 +152,7 @@
 
 
 def take_half(
-    place, half, got, state, last, mine, away, come, recv_sem, away_sem, come_sem, sign=None
+    place, half, got, state, first, last, mine, away, come, recv_sem, away_sem, come_sem, sign=None
 ):
     def keep(rows, block, core):
         product = by_last(rows, last[...])
@@ -158,7 +161,7 @@
             where = pl.ds(pl.multiple_of(dev * 8, 8), 8)
             for h in range(HALF):
                 row = (step * HALF + h) * 8
-                state[half * HALF + h, where, :] = product[row : row + 8]
+                state[first + h, where, :] = product[row : row + 8]
 
     def forward(block):
         slot = half * BLOCKS + block
@@ -204,10 +207,10 @@
 
 
 def window_kernel(
-    pairs, gates, x, half_done,
+    pairs, gates, x, first, second,
     x_here, gates_here, wide, state, other, mine, row_sign,
     tiles_one, got_one, tiles_two, got_two, away_one, come_one, away_two, come_two,
-    x_sem, gate_sem, out_sem, send_sem, recv_one, recv_two, away_sem, come_sem_one, come_sem_two, ready,
+    x_sem, gate_sem, send_sem, recv_one, recv_two, away_sem, come_sem_one, come_sem_two, ready,
 ):
     place = Place()
 
@@ -269,7 +272,9 @@
         return carry
 
     def send_body(number, carry):
-        send_block(place, 0, BLOCKS - 1 - number, tiles_one, got_one, send_sem.at[0], recv_one)
+        send_block(
+            place, 0, BLOCKS - 1 - number, tiles_one, got_one, send_sem.at[0], recv_one
+        )
         return carry
 
     layer_one(0)
@@ -295,7 +300,7 @@
 
     for half in range(2):
         take_half(
-            place, half, got_one, other, wide.at[1], mine, away_one, come_one,
+            place, half, got_one, other, half * HALF, wide.at[1], mine, away_one, come_one,
             recv_one, away_sem.at[0], come_sem_one, sign_one[half],
         )
         for h in range(half * HALF, half * HALF + HALF):
@@ -303,23 +308,13 @@
         send_half(
             place, half, state, tiles_two, got_two, send_sem.at[1], recv_two, sign_two[half]
         )
-    out_copies = []
-    for half in range(2):
+    for half, target in enumerate((first, second)):
         take_half(
-            place, half, got_two, other, wide.at[3], mine, away_two, come_two,
+            place, half, got_two, other, half * HALF, wide.at[3], mine, away_two, come_two,
             recv_two, away_sem.at[1], come_sem_two,
         )
-        source = other
-        if half == 0:
-            source = x_here
-            for h in range(HALF):
-                x_here[h] = by_middle(wide[2], other[h])
-        out_copies.append(
-            pltpu.make_async_copy(
-                source.at[halves[half]], half_done.at[halves[half]], out_sem.at[half]
-            )
-        )
-        out_copies[half].start()
+        for h in range(HALF):
+            target[h] = by_middle(wide[2], other[half * HALF + h])
 
     most = pl.ds(0, CHIPS - 1)
     for number, (tiles, away) in enumerate(((tiles_one, away_one), (tiles_two, away_two))):
@@ -327,40 +322,27 @@
             part = tiles.at[half, most]
             pltpu.make_async_copy(part, part, send_sem.at[number]).wait()
         pltpu.make_async_copy(away, away, away_sem.at[number]).wait()
-    for copy in out_copies:
-        copy.wait()
-
-
-def last_kernel(half_done, gates, out, half_here, gate_here, out_here, gate_sem, in_sem, out_sem):
-    gate_copy = pltpu.make_async_copy(gates.at[2, 0], gate_here, gate_sem)
-    gate_copy.start()
+
+
+def leave_kernel(first, second, out, out_sem):
     copies = []
-    for half in (1, 0):
-        levels = pl.ds(half * HALF, HALF)
-        copies.append(
-            pltpu.make_async_copy(half_done.at[levels], half_here.at[levels], in_sem.at[half])
-        )
-        copies[-1].start()
-    gate_copy.wait()
-    middle = split_gate(gate_here[...])
+    for number, part in enumerate((first, second)):
+        for piece in range(2):
+            here = pl.ds(piece * 2, 2)
+            there = pl.ds(number * HALF + piece * 2, 2)
+            copies.append(
+                pltpu.make_async_copy(part.at[here], out.at[there], out_sem.at[number * 2 + piece])
+            )
+            copies[-1].start()
     for copy in copies:
         copy.wait()
-    finished = pl.ds(0, HALF)
-    copies = [pltpu.make_async_copy(half_here.at[finished], out.at[finished], out_sem.at[0])]
-    copies[0].start()
-    for h in range(HALF):
-        out_here[h] = by_middle(middle, half_here[HALF + h])
-        copies.append(
-            pltpu.make_async_copy(out_here.at[h], out.at[HALF + h], out_sem.at[1 + h])
-        )
-        copies[-1].start()
-    for copy in copies:
-        copy.wait()
-
-
+
+
+VMEM = pl.BlockSpec(memory_space=pltpu.VMEM)
 SMEM = pl.BlockSpec(memory_space=pltpu.SMEM)
 ANY = pl.BlockSpec(memory_space=pl.ANY)
 STATE = jax.ShapeDtypeStruct((HIGH, GATE, GATE), jnp.float32)
+PART = jax.ShapeDtypeStruct((HALF, GATE, GATE), jnp.float32)
 
 
 def per_device(amplitudes, joined_gates, pair_qubits):
@@ -369,11 +351,11 @@
     tiles = pltpu.VMEM((2, CHIPS, 8, 128), jnp.float32)
     within = pltpu.VMEM((2 * BLOCKS, 128, GATE), jnp.float32)
     dma = pltpu.SemaphoreType.DMA
-    half_done = pl.pallas_call(
+    first, second = pl.pallas_call(
         window_kernel,
-        out_shape=STATE,
+        out_shape=(PART, PART),
         in_specs=[SMEM, ANY, ANY],
-        out_specs=ANY,
+        out_specs=(VMEM, VMEM),
         scratch_shapes=[
             held,
             pltpu.VMEM((3, 2, GATE, GATE), jnp.float32),
@@ -393,7 +375,6 @@
             dma((2,)),
             dma,
             dma((2,)),
-            dma((2,)),
             dma((2 * BLOCKS,)),
             dma((2 * BLOCKS,)),
             dma((2,)),
@@ -403,26 +384,19 @@
         ],
         name="window",
         compiler_params=pltpu.CompilerParams(
-            collective_id=0, has_side_effects=True, vmem_limit_bytes=56 * 2**20
+            collective_id=0, has_side_effects=True, vmem_limit_bytes=51 * 2**20
         ),
         cost_estimate=pl.CostEstimate(flops=5 * 2**29, bytes_accessed=2**23, transcendentals=0),
     )(pair_qubits.transpose(0, 2, 1), joined_gates, state)
     out = pl.pallas_call(
-        last_kernel,
+        leave_kernel,
         out_shape=STATE,
-        in_specs=[ANY, ANY],
+        in_specs=[VMEM, VMEM],
         out_specs=ANY,
-        scratch_shapes=[
-            held,
-            pltpu.VMEM((GATE, GATE), jnp.float32),
-            pltpu.VMEM((HALF, GATE, GATE), jnp.float32),
-            dma,
-            dma((2,)),
-            dma((1 + HALF,)),
-        ],
-        name="last_product",
-        compiler_params=pltpu.CompilerParams(vmem_limit_bytes=56 * 2**20),
-    )(half_done, joined_gates)
+        scratch_shapes=[dma((4,))],
+        name="leave",
+        compiler_params=pltpu.CompilerParams(vmem_limit_bytes=51 * 2**20),
+    )(first, second)
     return out.reshape(amplitudes.shape)
 
 

time: 122 us -> 120 us (0.984)
  Pallas kernels: 122 us -> 120 us
    pallas_call x2, Pallas kernels: 122 us -> 120 us  [the longest x1 118 us: per_device(): pl.pallas_call(window_kernel, out_shape=(PART, PART), in_specs=[SMEM, ANY...]
where the time goes in v5:
time: 120 us
  Pallas kernels  120 us (100%)
    pallas_call x1, Pallas kernels, per_device(): pl.pallas_call(window_kernel, out_shape=(PART, PART), in_specs=[SMEM, ANY...  118 us

profile of v5, /device:TPU:1, one launch (start us, length us, event | category | flops | bytes accessed | tf_op | source)
XLA Modules:
  0.0 120.2 jit_solution(431507649364737743)
XLA Ops:
  0.0 0.0 copy-start
  0.0 0.7 copy-done
  0.7 118.2 %window.1 = (f32[4,256,256]{2,1,0:T(8,128)S(1)}, f32[4,256,256]{2,1,0:T(8,128)S(1)}) custom-call(s32[3,2,8]{2,1,0:T(2,128)S(1)} %bitcast.3, f32[3,2,256,256]{3,2,1,0:T(8,128)} %gates.1, f32[8,256,256]{2,1,0:T(8,128)} %bitcast.4), custom_call_target="tpu_custom_call" | custom-call | flops 2684354560 | bytes 8388608 | tf_op jit(solution)/shard_map/window/pallas_call | solution.py:354
  118.9 1.3 %leave.1 = f32[8,256,256]{2,1,0:T(8,128)} custom-call(f32[4,256,256]{2,1,0:T(8,128)S(1)} %get-tuple-element.7.first, f32[4,256,256]{2,1,0:T(8,128)S(1)} %get-tuple-element.8.second), custom_call_target="tpu_custom_call" | custom-call | tf_op jit(solution)/shard_map/leave/pallas_call | solution.py:391
Async XLA Ops:
  0.0 0.7 copy-start

commit v6 on v5

--- a/solution.py
+++ b/solution.py
@@ -121,9 +121,9 @@
     ).start()
 
 
-def send_block(place, half, block, tiles, got, send_sem, recv_sem):
+def send_block(place, half, block, tiles, got, send_sem, recv_sem, near_last=False):
     def send(step, inner):
-        grp, paired = place.partner(block, step, half == 1)
+        grp, paired = place.partner(block, step, near_last)
 
         @pl.when(grp * PAIRED + paired != place.chip)
         def _():
@@ -140,11 +140,11 @@
     ).start()
 
 
-def send_half(place, half, state, tiles, got, send_sem, recv_sem, sign=None):
+def send_half(place, half, state, tiles, got, send_sem, recv_sem, sign=None, near_last=False):
     def block_body(number, carry):
         block = BLOCKS - 1 - number
         pack_block(place, half, block, state, tiles, sign)
-        send_block(place, half, block, tiles, got, send_sem, recv_sem)
+        send_block(place, half, block, tiles, got, send_sem, recv_sem, near_last)
         return carry
 
     lax.fori_loop(0, BLOCKS, block_body, 0)
@@ -207,33 +207,31 @@
 
 
 def window_kernel(
-    pairs, gates, x, first, second,
-    x_here, gates_here, wide, state, other, mine, row_sign,
+    pairs_there, gates, x, first, second,
+    pairs, x_here, gates_here, wide, state, other, mine, row_sign,
     tiles_one, got_one, tiles_two, got_two, away_one, come_one, away_two, come_two,
-    x_sem, gate_sem, send_sem, recv_one, recv_two, away_sem, come_sem_one, come_sem_two, ready,
+    pair_sem, x_sem, gate_sem, send_sem, recv_one, recv_two, away_sem, come_sem_one, come_sem_two, ready,
 ):
     place = Place()
+    pair_copy = pltpu.make_async_copy(pairs_there, pairs, pair_sem)
+    pair_copy.start()
 
     barrier = pltpu.get_barrier_semaphore()
 
-    def greet_plane(step, carry):
-        grp, paired = place.at(step % 4, step // 4, 0)
+    def tell(semaphore, dx, dy, dz):
+        grp, paired = place.at(dx, dy, dz)
         pl.semaphore_signal(
-            barrier, inc=1, device_id=(grp, paired * 2 + place.core), device_id_type=MESH
-        )
-        return carry
+            semaphore, inc=1, device_id=(grp, paired * 2 + place.core), device_id_type=MESH
+        )
 
     def tell_line(semaphore):
-        def body(step, carry):
-            grp, paired = place.at(0, 0, step)
-            pl.semaphore_signal(
-                semaphore, inc=1, device_id=(grp, paired * 2 + place.core), device_id_type=MESH
-            )
-            return carry
-
-        lax.fori_loop(1, 8, body, 0)
-
-    lax.fori_loop(1, 32, greet_plane, 0)
+        for dz in (4, 3, 5, 2, 6, 1, 7):
+            tell(semaphore, 0, 0, dz)
+
+    plane = [(dx, dy) for dx in range(4) for dy in range(8) if dx + dy > 0]
+    plane.sort(key=lambda at: -min(at[0], 4 - at[0]) - min(at[1], 8 - at[1]))
+    for dx, dy in plane:
+        tell(barrier, dx, dy, 0)
     tell_line(barrier)
     pl.semaphore_signal(
         barrier, inc=1, device_id=(place.grp, place.sibling), device_id_type=MESH
@@ -249,6 +247,7 @@
     for copy in x_copies:
         copy.start()
 
+    pair_copy.wait()
     base = sign_of(iota((GATE, GATE), 0) * 256 + iota((GATE, GATE), 1), pairs, 0)
     rows = iota((GATE, 128), 0) * 256
     row_sign[...] = sign_of((iota((GATE, 128), 1) % 8) * 65536 + rows, pairs, 0) * sign_of(rows, pairs, 0)
@@ -306,7 +305,8 @@
         for h in range(half * HALF, half * HALF + HALF):
             state[h] = by_middle(wide[0], other[h])
         send_half(
-            place, half, state, tiles_two, got_two, send_sem.at[1], recv_two, sign_two[half]
+            place, half, state, tiles_two, got_two, send_sem.at[1], recv_two, sign_two[half],
+            near_last=half == 1,
         )
     for half, target in enumerate((first, second)):
         take_half(
@@ -339,7 +339,6 @@
 
 
 VMEM = pl.BlockSpec(memory_space=pltpu.VMEM)
-SMEM = pl.BlockSpec(memory_space=pltpu.SMEM)
 ANY = pl.BlockSpec(memory_space=pl.ANY)
 STATE = jax.ShapeDtypeStruct((HIGH, GATE, GATE), jnp.float32)
 PART = jax.ShapeDtypeStruct((HALF, GATE, GATE), jnp.float32)
@@ -354,9 +353,10 @@
     first, second = pl.pallas_call(
         window_kernel,
         out_shape=(PART, PART),
-        in_specs=[SMEM, ANY, ANY],
+        in_specs=[ANY, ANY, ANY],
         out_specs=(VMEM, VMEM),
         scratch_shapes=[
+            pltpu.SMEM((3, 2, 8), jnp.int32),
             held,
             pltpu.VMEM((3, 2, GATE, GATE), jnp.float32),
             pltpu.VMEM((4, GATE, 3 * GATE), jnp.bfloat16),
@@ -372,6 +372,7 @@
             within,
             within,
             within,
+            dma,
             dma((2,)),
             dma,
             dma((2,)),

time: 120 us -> 119 us (level)
  Pallas kernels: 120 us -> 118 us
    pallas_call x1, Pallas kernels: 118 us -> 117 us  [per_device(): pl.pallas_call(window_kernel, out_shape=(PART, PART), in_specs=[ANY, ANY,...]
where the time goes in v6:
time: 119 us
  Pallas kernels  118 us (99%)
    pallas_call x1, Pallas kernels, per_device(): pl.pallas_call(window_kernel, out_shape=(PART, PART), in_specs=[ANY, ANY,...  117 us

profile of v6, /device:TPU:1, one launch (start us, length us, event | category | flops | bytes accessed | tf_op | source)
XLA Modules:
  0.0 118.6 jit_solution(17203633361549789565)
XLA Ops:
  0.0 0.0 copy-start
  0.0 0.7 copy-done
  0.7 116.6 %window.1 = (f32[4,256,256]{2,1,0:T(8,128)S(1)}, f32[4,256,256]{2,1,0:T(8,128)S(1)}) custom-call(s32[3,2,8]{2,1,0:T(2,128)S(1)} %bitcast.3, f32[3,2,256,256]{3,2,1,0:T(8,128)} %gates.1, f32[8,256,256]{2,1,0:T(8,128)} %bitcast.4), custom_call_target="tpu_custom_call" | custom-call | flops 2684354560 | bytes 8388608 | tf_op jit(solution)/shard_map/window/pallas_call | solution.py:353
  117.3 1.3 %leave.1 = f32[8,256,256]{2,1,0:T(8,128)} custom-call(f32[4,256,256]{2,1,0:T(8,128)S(1)} %get-tuple-element.7.first, f32[4,256,256]{2,1,0:T(8,128)S(1)} %get-tuple-element.8.second), custom_call_target="tpu_custom_call" | custom-call | tf_op jit(solution)/shard_map/leave/pallas_call | solution.py:392
Async XLA Ops:
  0.0 0.7 copy-start
